TPU v7x, 32 devices: a whole 2x2x4 slice. The times are simulated.
32 devices in a mesh: rep: 2 (over x), node: 4 (over z), local: 4 (over y, core).
Axes of the slice: x: 2, y: 2, z: 4, core: 2. Of those that a mesh axis runs over, the one named last changes fastest.
Arguments:
- tokens: bfloat16 [2048, 7168], P(('rep', 'node', 'local')), parts along dimension 0, may hold values from -6 to 6
- expert_ids: int32 [2048, 2], P(('rep', 'node', 'local')), parts along dimension 0, may hold values from 0 to 7, as said below
- gate_values: bfloat16 [2048, 2], P(('rep', 'node', 'local')), parts along dimension 0, may hold values from 0.049804688 to 0.59765625
- w_gate: bfloat16 [16, 7168, 1024], P(('node', 'local')), may hold values from -0.0625 to 0.0625
- w_up: bfloat16 [16, 7168, 1024], P(('node', 'local')), may hold values from -0.0625 to 0.0625
- w_down: bfloat16 [16, 1024, 7168], P(('node', 'local')), may hold values from -0.125 to 0.125
Outputs:
- mixed: bfloat16 [2048, 7168], P(('rep', 'node', 'local')), parts along dimension 0
There are 2 independent parts, one for each index of `rep`. A program takes and returns all parts, laid end to end along the dimension named above; an argument that names none is the same for every part. Nothing has to cross between parts.
Inputs may be any that keep to these rules, and one draw needn't show every extreme that they name: `expert_ids`: each token names 2 different experts (expert e lies on node e // 2): half of the tokens of one device name both experts of one node, the other half one expert on each of two different nodes. Among the 64 tokens of one device (aligned blocks of rows), exactly 24 reach each node.
All inputs are finite; a program needn't handle non-finite values.
Results may differ from a plain program's by a relative error of at most 0.008.
Values may be sent and summed in bfloat16 or wider, within the bound.
A program may use at most 192 MiB of HBM per device.

v0:
```python
import jax
import jax.numpy as jnp
from jax import lax
from jax.sharding import PartitionSpec as P

EXP_NODE = 2


def local(tokens, expert_ids, gate_values, w_gate, w_up, w_down):
    nodes = lax.axis_size("node")
    lanes = lax.axis_size("local")
    split = lanes // EXP_NODE
    width = tokens.shape[1]
    count_tok = tokens.shape[0]
    capacity = 3 * count_tok // (2 * nodes)
    node_labels = jnp.arange(nodes, dtype=jnp.int32)
    owner = expert_ids // EXP_NODE
    reached = jnp.any(owner[:, :, None] == node_labels[None, None, :], axis=1).astype(jnp.int32)
    before = jnp.cumsum(reached, axis=0) - reached
    slot_labels = jnp.arange(capacity, dtype=jnp.int32)
    picked = (before.T[:, None, :] == slot_labels[None, :, None]) & (reached.T[:, None, :] == 1)
    selection = picked.reshape(nodes * capacity, count_tok).astype(jnp.bfloat16)
    send_rows = (
        jnp.dot(selection, tokens, preferred_element_type=jnp.float32)
        .astype(jnp.bfloat16)
        .reshape(nodes, capacity, width)
    )
    expert_labels = jnp.arange(nodes * EXP_NODE, dtype=jnp.int32)
    matches = expert_ids[:, :, None] == expert_labels[None, None, :]
    gate_table = jnp.sum(
        jnp.where(matches, gate_values.astype(jnp.float32)[:, :, None], jnp.float32(0.0)), axis=1
    )
    gate_table = gate_table.reshape(count_tok, nodes, EXP_NODE)
    slot_gates = jnp.einsum("mct,tmk->mck", picked.astype(jnp.float32), gate_table).astype(
        jnp.bfloat16
    )
    arrived, arrived_gates = (
        lax.all_to_all(send_rows, "node", split_axis=0, concat_axis=0, tiled=True),
        lax.all_to_all(slot_gates, "node", split_axis=0, concat_axis=0, tiled=True),
    )
    gathered, gathered_gates = (
        lax.all_gather(arrived, "local", axis=0, tiled=True),
        lax.all_gather(arrived_gates, "local", axis=0, tiled=True),
    )
    rows_all = gathered.reshape(-1, width)
    gates_all = gathered_gates.reshape(-1, EXP_NODE)
    which = lax.axis_index("local") // split
    own_gate = lax.dynamic_slice_in_dim(gates_all, which, 1, 1).astype(jnp.float32)
    gate = jnp.dot(rows_all, w_gate[0], preferred_element_type=jnp.float32)
    upper = jnp.dot(rows_all, w_up[0], preferred_element_type=jnp.float32)
    gated = (own_gate * jax.nn.silu(gate) * upper).astype(jnp.bfloat16)
    down_w = w_down[0]
    own_rows = lax.psum_scatter(
        jnp.dot(gated, down_w, preferred_element_type=jnp.float32).astype(jnp.bfloat16),
        "local",
        scatter_dimension=0,
        tiled=True,
    )
    returned = lax.all_to_all(
        own_rows.reshape(nodes, capacity, width), "node", split_axis=0, concat_axis=0, tiled=True
    )
    mixed = jnp.dot(
        selection.T, returned.reshape(nodes * capacity, width), preferred_element_type=jnp.float32
    )
    return mixed.astype(jnp.bfloat16)


def solution(mesh):
    placed = (
        P(("rep", "node", "local"), None),
        P(("rep", "node", "local"), None),
        P(("rep", "node", "local"), None),
        P(("node", "local"), None, None),
        P(("node", "local"), None, None),
        P(("node", "local"), None, None),
    )
    return jax.shard_map(
        local,
        mesh=mesh,
        in_specs=placed,
        out_specs=P(("rep", "node", "local"), None),
        check_vma=False,
    )
```

profile of v0, /device:TPU:0, one launch (start us, length us, event | category | flops | bytes accessed | tf_op | source)
XLA Modules:
  0.0 215.8 jit_solution(7256979981681480240)
XLA Ops:
  6.5 0.0 copy-start
  6.5 0.0 all-gather.2.cloned.1.call-start
  6.5 0.8 and_select_fusion
  7.3 0.1 eq.74
  7.4 0.1 copy.24
  7.5 0.1 copy.26
  7.6 0.1 reduce_window_sum.11
  7.7 0.1 copy.25
  7.8 0.1 fusion.15
  7.9 0.0 copy-done
  7.9 0.0 copy-start.3
  7.9 0.0 copy-start.1
  8.0 0.5 convolution_convert_fusion
  8.5 39.0 %all_to_all.15 = bf16[4,24,7168]{2,1,0:T(8,128)(2,1)} all-to-all(bf16[4,24,7168]{2,1,0:T(8,128)(2,1)S(1)} %bitcast.40), channel_id=1, replica_groups=mesh['rep'=2,'node'=4,'local'=4] {'node'}, dimensions={0} | all-to-all | bytes 2752512 | tf_op jit(solution)/shard_map/all_to_all | solution.py:38
  47.4 0.0 all-gather.2.cloned.1.call-update
  47.5 0.0 copy-done.3
  47.5 0.0 copy-done.1
  47.5 0.7 convolution_convert_fusion.1
  48.2 3.2 %all-to-all-start = ((bf16[4,24,2]{1,2,0:T(2,128)(2,1)}), bf16[4,24,2]{1,2,0:T(2,128)(2,1)S(1)}, u32[]{:S(2)}, u32[]{:S(2)}) async-start(bf16[4,24,2]{1,2,0:T(2,128)(2,1)} %convolution_convert_fusion.1), calls=%async_computation | async-start | bytes 4096 | tf_op jit(solution)/shard_map/all_to_all | solution.py:39
  51.4 0.0 reduce-scatter.2.cloned.1.call-start
  51.5 5.4 %all-to-all-done = bf16[4,24,2]{1,2,0:T(2,128)(2,1)S(1)} async-done(((bf16[4,24,2]{1,2,0:T(2,128)(2,1)}), bf16[4,24,2]{1,2,0:T(2,128)(2,1)S(1)}, u32[]{:S(2)}, u32[]{:S(2)}) %all-to-all-start) | async-done | bytes 416 | tf_op jit(solution)/shard_map/all_to_all | solution.py:39
  56.9 5.2 %all_gather.6 = bf16[16,24,2]{1,2,0:T(2,128)(2,1)S(1)} all-gather(bf16[4,24,2]{1,2,0:T(2,128)(2,1)S(1)} %all-to-all-done), channel_id=1, replica_groups=mesh['rep'=2,'node'=4,'local'=4] {'local'}, dimensions={0}, use_global_device_ids=true | all-gather | bytes 1920 | tf_op jit(solution)/shard_map/all_gather | solution.py:43
  62.1 0.1 reshape.27
  62.2 26.5 %all-gather.2.cloned.1.call-done = bf16[16,24,7168]{2,1,0:T(8,128)(2,1)} async-done(((bf16[4,24,7168]{2,1,0:T(8,128)(2,1)}), bf16[16,24,7168]{2,1,0:T(8,128)(2,1)}) %all-gather.2.cloned.1.call-update) | async-done | bytes 5505040 | tf_op jit(solution)/shard_map/all_gather | solution.py:42
  88.7 0.0 copy-start.2
  88.7 0.0 slice-start
  88.7 0.0 slice-start.1
  88.7 0.0 slice-start.2
  88.7 10.8 %fusion.4 = f32[384,1024]{1,0:T(8,128)S(1)} fusion(bf16[384,7168]{1,0:T(8,128)(2,1)} %bitcast.45, bf16[1,7168,1024]{2,1,0:T(8,128)(2,1)} %param.9), kind=kOutput, calls=%fused_computation.4 | convolution fusion | flops 5637144576 | bytes 21757952 | tf_op jit(solution)/shard_map/dot_general | solution.py:49
  99.6 0.0 copy-done.2
  99.6 0.0 slice-start.3
  99.6 9.6 %multiply_convert_fusion = bf16[384,1024]{1,0:T(8,128)(2,1)S(1)} fusion(f32[384,1024]{1,0:T(8,128)S(1)} %fusion.4, bf16[384,7168]{1,0:T(8,128)(2,1)S(1)} %bitcast.46, bf16[1,7168,1024]{2,1,0:T(8,128)(2,1)} %param.10, f32[384]{0:T(512)S(1)} %convert_reduce_fusion), kind=kOutput, calls=%fused_computation.10 | convolution fusion | flops 5639897088 | bytes 22545920 | tf_op jit(solution)/shard_map/dot_general | solution.py:50
  109.2 0.0 slice-done
  109.2 0.0 slice-done.1
  109.2 0.0 slice-done.2
  109.2 0.0 slice-done.3
  109.2 7.7 %fusion.6 = bf16[384,7168]{1,0:T(8,128)(2,1)} fusion(bf16[384,1024]{1,0:T(8,128)(2,1)S(1)} %multiply_convert_fusion, bf16[1,1024,7168]{2,1,0:T(8,128)(2,1)S(1)} %bitcast.44), kind=kOutput, calls=%fused_computation.6 | convolution fusion | flops 5639897088 | bytes 20971520 | tf_op jit(solution)/shard_map/dot_general | solution.py:54
  117.0 0.0 reduce-scatter.2.cloned.1.call-update
  117.0 53.3 %reduce-scatter.2.cloned.1.call-done = bf16[96,7168]{1,0:T(8,128)(2,1)} async-done(((bf16[384,7168]{1,0:T(8,128)(2,1)}), bf16[96,7168]{1,0:T(8,128)(2,1)}) %reduce-scatter.2.cloned.1.call-update) | async-done | bytes 1376272 | tf_op jit(solution)/shard_map/reduce_scatter | solution.py:53
  170.3 37.3 %all_to_all.16 = bf16[4,24,7168]{2,1,0:T(8,128)(2,1)S(1)} all-to-all(bf16[4,24,7168]{2,1,0:T(8,128)(2,1)} %bitcast.41), channel_id=1, replica_groups=mesh['rep'=2,'node'=4,'local'=4] {'node'}, dimensions={0} | all-to-all | bytes 2752512 | tf_op jit(solution)/shard_map/all_to_all | solution.py:59
  207.6 1.4 fusion.9
  (9 shorter events, 0.1 us)
Async XLA Ops:
  6.5 1.4 copy-start
  6.5 82.2 %all-gather.2.cloned.1.call-start = ((), (), s32[]{:S(2)}) async-start(), calls=%async_computation.4 | async-start | bytes 6881280 | tf_op jit(solution)/shard_map/all_gather | solution.py:42
  7.9 39.5 %copy-start.3 = (bf16[64,2]{0,1:T(2,128)(2,1)S(1)}, bf16[64,2]{0,1:T(2,128)(2,1)}, u32[]{:S(2)}) copy-start(bf16[64,2]{0,1:T(2,128)(2,1)} %param.8) | copy-start | bytes 772
  7.9 39.5 %copy-start.1 = (s32[64,2]{0,1:T(2,128)S(1)}, s32[64,2]{0,1:T(2,128)}, u32[]{:S(2)}) copy-start(s32[64,2]{0,1:T(2,128)} %param.7) | copy-start | bytes 1540
  48.2 8.7 %all-to-all-start = ((bf16[4,24,2]{1,2,0:T(2,128)(2,1)}), bf16[4,24,2]{1,2,0:T(2,128)(2,1)S(1)}, u32[]{:S(2)}, u32[]{:S(2)}) async-start(bf16[4,24,2]{1,2,0:T(2,128)(2,1)} %convolution_convert_fusion.1), calls=%async_computation | async-start | bytes 4096 | tf_op jit(solution)/shard_map/all_to_all | solution.py:39
  51.4 118.8 %reduce-scatter.2.cloned.1.call-start = ((), (), s32[]{:S(2)}) async-start(), calls=%async_computation.5 | async-start | bytes 6881280 | tf_op jit(solution)/shard_map/reduce_scatter | solution.py:53
  88.7 10.8 %copy-start.2 = (bf16[16,24,7168]{2,1,0:T(8,128)(2,1)S(1)}, bf16[16,24,7168]{2,1,0:T(8,128)(2,1)}, u32[]{:S(2)}) copy-start(bf16[16,24,7168]{2,1,0:T(8,128)(2,1)} %all-gather.2.cloned.1.call-done) | copy-start | bytes 16515076
  88.7 20.5 %slice-start = ((s8[14680064]{0:T(1024)(128)(4,1)}), s8[4194304]{0:T(1024)(128)(4,1)S(1)}, s32[]{:S(2)}) async-start(s8[14680064]{0:T(1024)(128)(4,1)} %bitcast.43), calls=%async_computation.6 | async-start | bytes 8388608
  88.7 20.5 %slice-start.1 = ((s8[14680064]{0:T(1024)(128)(4,1)}), s8[4194304]{0:T(1024)(128)(4,1)S(1)}, s32[]{:S(2)}) async-start(s8[14680064]{0:T(1024)(128)(4,1)} %bitcast.43), calls=%async_computation.7 | async-start | bytes 8388608
  88.7 20.5 %slice-start.2 = ((s8[14680064]{0:T(1024)(128)(4,1)}), s8[4194304]{0:T(1024)(128)(4,1)S(1)}, s32[]{:S(2)}) async-start(s8[14680064]{0:T(1024)(128)(4,1)} %bitcast.43), calls=%async_computation.8 | async-start | bytes 8388608
  99.6 9.6 %slice-start.3 = ((s8[14680064]{0:T(1024)(128)(4,1)}), s8[2097152]{0:T(1024)(128)(4,1)S(1)}, s32[]{:S(2)}) async-start(s8[14680064]{0:T(1024)(128)(4,1)} %bitcast.43), calls=%async_computation.9 | async-start | bytes 4194304
Sparse Core Ops, SparseCore 0:
  47.6 41.0 all-gather.1
  117.1 53.1 reduce-scatter.1
where the time goes:
time: 216 us
  waiting for transfers between devices  85.2 us (39%)
  blocking collectives  81.5 us (38%)
  matrix products  30.8 us (14%)
  between operations  13.6 us (6%)
  starting transfers between devices  3.27 us (2%)
    reduce_scatter x1, waiting for transfers between devices, local(): lax.psum_scatter(jnp.dot(gated, down_w, preferred_element_type=jnp.float3...  53.3 us
    all_to_all x1, blocking collectives, local(): lax.all_to_all(send_rows, 'node', split_axis=0, concat_axis=0, tiled=True)  39 us
    all_to_all x1, blocking collectives, local(): lax.all_to_all(own_rows.reshape(nodes, capacity, width), 'node', split_ax...  37.3 us
    all_gather x1, waiting for transfers between devices, local(): lax.all_gather(arrived, 'local', axis=0, tiled=True)  26.5 us
    dot_general x1, matrix products, local(): gate = jnp.dot(rows_all, w_gate[0], preferred_element_type=jnp.float32)  10.8 us
    dot_general x1, matrix products, local(): upper = jnp.dot(rows_all, w_up[0], preferred_element_type=jnp.float32)  9.58 us
    dot_general x1, matrix products, local(): jnp.dot(gated, down_w, preferred_element_type=jnp.float32)  7.75 us
    all_to_all x1, waiting for transfers between devices, local(): lax.all_to_all(slot_gates, 'node', split_axis=0, concat_axis=0, tiled=True)  5.37 us
  transfers between devices with their start and end apart: 3, of which 3 were waited for; matrix products, arithmetic and copies ran while one was open for 0% of the time, Pallas kernels for 0%

commit v1 on v0

--- a/solution.py
+++ b/solution.py
@@ -1,9 +1,354 @@
+import functools
+
 import jax
 import jax.numpy as jnp
 from jax import lax
+from jax.experimental import pallas as pl
+from jax.experimental.pallas import tpu as pltpu
 from jax.sharding import PartitionSpec as P
 
 EXP_NODE = 2
+MESH = pl.DeviceIdType.MESH
+F32 = jnp.float32
+BF16 = jnp.bfloat16
+LANES = 128
+GATE_TILE = 256
+TILE = 512
+NT = (((1,), (1,)), ((), ()))
+
+TOK, TBL, OUT, Z, Y, C1, C2, RC, RY, RZ = 0, 1, 2, 4, 8, 12, 16, 20, 24, 28
+SEMS = 32
+
+
+def fused_kernel(
+    cap,
+    tokens,
+    ids_t,
+    gates_t,
+    w_gate,
+    w_up,
+    w_down,
+    out,
+    wg,
+    wu,
+    wd,
+    x,
+    sendz,
+    tok_n,
+    tbl,
+    rows_before,
+    rows_reached,
+    sel,
+    hid,
+    crecv,
+    yrecv,
+    zret,
+    load_sem,
+    send_sem,
+    recv_sem,
+):
+    half = tokens.shape[1] // 2
+    count_tok = tokens.shape[0]
+    pair = 2 * cap
+    ff = wg.shape[1]
+    me = lax.axis_index("node")
+    lane = lax.axis_index("local")
+    y = lane // 2
+    c = lane % 2
+    core_nbr = {"local": lane + 1 - 2 * c}
+    y_nbr = {"local": (lane + 2) % 4}
+    node_of = [me, me + 1 - 2 * (me % 2), (me + 2) % 4, 3 - me]
+
+    loads = [
+        pltpu.make_async_copy(src.at[0], dst, load_sem.at[i])
+        for i, (src, dst) in enumerate(((w_gate, wg), (w_up, wu), (w_down, wd)))
+    ]
+    barrier = pltpu.get_barrier_semaphore()
+    partners = [core_nbr, y_nbr] + [{"node": node_of[k]} for k in (1, 2, 3)]
+    for partner in partners:
+        pl.semaphore_signal(barrier, inc=1, device_id=partner, device_id_type=MESH)
+    pl.semaphore_wait(barrier, len(partners))
+
+    def remote(src, dst, number, device):
+        return pltpu.make_async_remote_copy(
+            src_ref=src,
+            dst_ref=dst,
+            send_sem=send_sem.at[number],
+            recv_sem=recv_sem.at[number],
+            device_id=device,
+            device_id_type=MESH,
+        )
+
+    own_at = pl.multiple_of(c * half, LANES)
+    nbr_at = pl.multiple_of((1 - c) * half, LANES)
+    tok_copy = remote(tokens.at[:, pl.ds(nbr_at, half)], tok_n, TOK, core_nbr)
+    tok_copy.start()
+    row = lax.broadcasted_iota(jnp.int32, (LANES, count_tok), 0)
+    tbl[0] = jnp.where(ids_t[0:1, :] == row, gates_t[0:1, :], 0.0) + jnp.where(
+        ids_t[1:2, :] == row, gates_t[1:2, :], 0.0
+    )
+    tbl_copy = remote(tbl.at[0], tbl.at[1], TBL, core_nbr)
+    tbl_copy.start()
+
+    def select(which, first):
+        named = jnp.where(tbl[which] != 0.0, 1.0, 0.0).astype(BF16)
+        pool = jnp.where(
+            lax.broadcasted_iota(jnp.int32, (8, LANES), 1) // EXP_NODE
+            == lax.broadcasted_iota(jnp.int32, (8, LANES), 0),
+            1.0,
+            0.0,
+        ).astype(BF16)
+        reached = jnp.minimum(jnp.dot(pool, named, preferred_element_type=F32), 1.0)
+        upper = jnp.where(
+            lax.broadcasted_iota(jnp.int32, (count_tok, count_tok), 0)
+            < lax.broadcasted_iota(jnp.int32, (count_tok, count_tok), 1),
+            1.0,
+            0.0,
+        ).astype(BF16)
+        rows_before[...] = jnp.dot(reached.astype(BF16), upper, preferred_element_type=F32)
+        rows_reached[...] = reached
+        slot = lax.broadcasted_iota(jnp.int32, (pair, count_tok), 0)
+        for k in range(4):
+            before = rows_before[pl.ds(node_of[k], 1), :].astype(jnp.int32) + first
+            there = rows_reached[pl.ds(node_of[k], 1), :]
+            sel[which, k * pair : (k + 1) * pair, :] = jnp.where(
+                before == slot, there, 0.0
+            ).astype(BF16)
+
+    select(0, cap * c)
+    tbl_copy.wait_recv()
+    select(1, cap * (1 - c))
+    tok_copy.wait_recv()
+
+    def build(k, dst):
+        s_own = sel[0, k * pair : (k + 1) * pair, :]
+        s_nbr = sel[1, k * pair : (k + 1) * pair, :]
+        gates = lax.dot_general(
+            s_own, tbl[0].astype(BF16), NT, preferred_element_type=F32
+        ) + lax.dot_general(s_nbr, tbl[1].astype(BF16), NT, preferred_element_type=F32)
+        dst[:, half : half + LANES] = gates.astype(BF16)
+
+        @pl.loop(0, half // TILE)
+        def _(j):
+            at = pl.multiple_of(j * TILE, TILE)
+            here = pl.multiple_of(own_at + at, LANES)
+            got = jnp.dot(s_own, tokens[:, pl.ds(here, TILE)], preferred_element_type=F32)
+            got += jnp.dot(s_nbr, tok_n[:, pl.ds(at, TILE)], preferred_element_type=F32)
+            dst[:, pl.ds(at, TILE)] = got.astype(BF16)
+
+    def z_copy(k):
+        return remote(
+            sendz.at[k - 1], x.at[c, me, y], Z + k, {"node": node_of[k]}
+        )
+
+    def y_copy(k):
+        here = x.at[c, node_of[k], y]
+        return remote(here, here, Y + k, y_nbr)
+
+    def c1_copy(k):
+        here = x.at[c, node_of[k], y]
+        return remote(here, here, C1 + k, core_nbr)
+
+    def c2_copy(k):
+        here = x.at[c, node_of[k], 1 - y]
+        return remote(here, here, C2 + k, core_nbr)
+
+    def rc_copy(k):
+        return remote(
+            x.at[1 - c, node_of[k], :, :, pl.ds(0, half)], crecv.at[k], RC + k, core_nbr
+        )
+
+    def ry_copy(k):
+        return remote(crecv.at[k, 1 - y], yrecv.at[k], RY + k, y_nbr)
+
+    def rz_copy(k):
+        return remote(crecv.at[k, y], zret.at[k], RZ + k, {"node": node_of[k]})
+
+    def take_z(k):
+        if k > 0:
+            z_copy(k).wait_recv()
+        y_copy(k).start()
+        c1_copy(k).start()
+
+    def take_y(k):
+        y_copy(k).wait_recv()
+        c2_copy(k).start()
+
+    def compute(k):
+        m = node_of[k]
+        c1_copy(k).wait()
+        c2_copy(k).wait()
+        y_copy(k).wait_send()
+        count = 2 * pair
+        table = x[c, m, :, :, half : half + LANES].reshape(count, LANES).astype(F32)
+        mine = lax.broadcasted_iota(jnp.int32, (count, LANES), 1) == me * EXP_NODE + y
+        weight = jnp.sum(jnp.where(mine, table, 0.0), axis=1, keepdims=True)
+
+        @pl.loop(0, ff // GATE_TILE)
+        def _(j):
+            cols = pl.ds(pl.multiple_of(j * GATE_TILE, GATE_TILE), GATE_TILE)
+            x0 = x[0, m, :, :, :half].reshape(count, half)
+            x1 = x[1, m, :, :, :half].reshape(count, half)
+            gate = jnp.dot(x0, wg[:half, cols], preferred_element_type=F32)
+            gate += jnp.dot(x1, wg[half:, cols], preferred_element_type=F32)
+            upper = jnp.dot(x0, wu[:half, cols], preferred_element_type=F32)
+            upper += jnp.dot(x1, wu[half:, cols], preferred_element_type=F32)
+            hid[:, cols] = (weight * (gate / (1.0 + jnp.exp(-gate))) * upper).astype(BF16)
+
+        for h in range(2):
+
+            @pl.loop(0, half // TILE)
+            def _(j):
+                at = pl.multiple_of(j * TILE, TILE)
+                part = jnp.dot(
+                    hid[...], wd[:, pl.ds(pl.multiple_of(h * half + at, TILE), TILE)],
+                    preferred_element_type=F32,
+                )
+                x[h, m, :, :, pl.ds(at, TILE)] = part.astype(BF16).reshape(2, pair, TILE)
+
+        rc_copy(k).start()
+
+    def fold_core(k):
+        rc_copy(k).wait_recv()
+        crecv[k, 1 - y] = (
+            crecv[k, 1 - y].astype(F32) + x[c, node_of[k], 1 - y, :, :half].astype(F32)
+        ).astype(BF16)
+        ry_copy(k).start()
+
+    def fold_y(k):
+        ry_copy(k).wait_recv()
+        total = (
+            crecv[k, y].astype(F32)
+            + x[c, node_of[k], y, :, :half].astype(F32)
+            + yrecv[k].astype(F32)
+        ).astype(BF16)
+        if k == 0:
+            zret[0] = total
+        else:
+            crecv[k, y] = total
+            rz_copy(k).start()
+
+    build(2, sendz.at[1])
+    z_copy(2).start()
+    build(1, sendz.at[0])
+    z_copy(1).start()
+    build(0, x.at[c, me, y])
+    take_z(0)
+    for load in loads:
+        load.start()
+    build(3, sendz.at[2])
+    take_y(0)
+    z_copy(2).wait_send()
+    z_copy(3).start()
+    take_z(1)
+    take_z(2)
+    for load in loads:
+        load.wait()
+    compute(0)
+    take_y(1)
+    take_y(2)
+    fold_core(0)
+    compute(1)
+    take_z(3)
+    fold_core(1)
+    fold_y(0)
+    compute(2)
+    take_y(3)
+    fold_core(2)
+    fold_y(1)
+    compute(3)
+    fold_y(2)
+    fold_core(3)
+    fold_y(3)
+
+    eye = jnp.where(
+        lax.broadcasted_iota(jnp.int32, (count_tok, count_tok), 0)
+        == lax.broadcasted_iota(jnp.int32, (count_tok, count_tok), 1),
+        1.0,
+        0.0,
+    ).astype(BF16)
+    for k in (1, 2, 3):
+        rz_copy(k).wait_recv()
+    out_copy = remote(
+        tok_n, out.at[:, pl.ds(own_at, half)], OUT, core_nbr
+    )
+    for which in (1, 0):
+        back = lax.dot_general(eye, sel[which], NT, preferred_element_type=F32).astype(BF16)
+
+        @pl.loop(0, half // TILE)
+        def _(j):
+            at = pl.multiple_of(j * TILE, TILE)
+            got = zret[:, :, pl.ds(at, TILE)].reshape(4 * pair, TILE)
+            mixed = jnp.dot(back, got, preferred_element_type=F32).astype(BF16)
+            if which == 1:
+                tok_n[:, pl.ds(at, TILE)] = mixed
+            else:
+                out[:, pl.ds(pl.multiple_of(own_at + at, LANES), TILE)] = mixed
+
+        if which == 1:
+            out_copy.start()
+    out_copy.wait()
+    tok_copy.wait_send()
+    tbl_copy.wait_send()
+    z_copy(1).wait_send()
+    z_copy(3).wait_send()
+    for k in range(4):
+        rc_copy(k).wait_send()
+        ry_copy(k).wait_send()
+        if k > 0:
+            rz_copy(k).wait_send()
+
+
+def fused(tokens, expert_ids, gate_values, w_gate, w_up, w_down):
+    count_tok, width = tokens.shape
+    nodes = lax.axis_size("node")
+    cap = 3 * count_tok // (2 * nodes)
+    pair = 2 * cap
+    half = width // 2
+    ff = w_gate.shape[2]
+    vmem = pl.BlockSpec(memory_space=pltpu.VMEM)
+    hbm = pl.BlockSpec(memory_space=pl.ANY)
+    dma = pltpu.SemaphoreType.DMA
+    return pl.pallas_call(
+        functools.partial(fused_kernel, cap),
+        out_shape=jax.ShapeDtypeStruct((count_tok, width), BF16),
+        in_specs=[vmem, vmem, vmem, hbm, hbm, hbm],
+        out_specs=vmem,
+        scratch_shapes=[
+            pltpu.VMEM((width, ff), BF16),
+            pltpu.VMEM((width, ff), BF16),
+            pltpu.VMEM((ff, width), BF16),
+            pltpu.VMEM((2, nodes, 2, pair, half + LANES), BF16),
+            pltpu.VMEM((nodes - 1, pair, half + LANES), BF16),
+            pltpu.VMEM((count_tok, half), BF16),
+            pltpu.VMEM((2, LANES, count_tok), F32),
+            pltpu.VMEM((8, count_tok), F32),
+            pltpu.VMEM((8, count_tok), F32),
+            pltpu.VMEM((2, nodes * pair, count_tok), BF16),
+            pltpu.VMEM((2 * pair, ff), BF16),
+            pltpu.VMEM((nodes, 2, pair, half), BF16),
+            pltpu.VMEM((nodes, pair, half), BF16),
+            pltpu.VMEM((nodes, pair, half), BF16),
+            dma((3,)),
+            dma((SEMS,)),
+            dma((SEMS,)),
+        ],
+        compiler_params=pltpu.CompilerParams(
+            collective_id=0, has_side_effects=True, vmem_limit_bytes=61 * 1024 * 1024
+        ),
+        cost_estimate=pl.CostEstimate(
+            flops=12 * nodes * pair * width * ff,
+            bytes_accessed=6 * width * ff,
+            transcendentals=2 * nodes * pair * ff,
+        ),
+    )(
+        tokens,
+        expert_ids.T,
+        gate_values.astype(F32).T,
+        w_gate,
+        w_up,
+        w_down,
+    )
 
 
 def local(tokens, expert_ids, gate_values, w_gate, w_up, w_down):
@@ -74,8 +419,9 @@
         P(("node", "local"), None, None),
         P(("node", "local"), None, None),
     )
+    paired = mesh.shape["node"] == 4 and mesh.shape["local"] == 4
     return jax.shard_map(
-        local,
+        fused if paired else local,
         mesh=mesh,
         in_specs=placed,
         out_specs=P(("rep", "node", "local"), None),

time: 216 us -> 119 us (0.55)
  the two profiles are of different devices: /device:TPU:0 before, /device:TPU:21 now
where the time goes in v1:
time: 119 us; the launch traced here: 118 us
  Pallas kernels  115 us (97%)
  local copies, waits for them, and re-layouts  2.16 us (2%)
  other arithmetic  1.22 us (1%)
    pallas_call x1, Pallas kernels, fused(): pl.pallas_call(functools.partial(fused_kernel, cap), out_shape=jax.ShapeD...  115 us

profile of v1, /device:TPU:21, one launch (start us, length us, event | category | flops | bytes accessed | tf_op | source)
XLA Modules:
  0.0 118.4 jit_solution(379150947173959128)
XLA Ops:
  0.0 1.2 %convert_bitcast_fusion.gates_t = f32[2,64]{1,0:T(2,128)} fusion(bf16[64,2]{0,1:T(2,128)(2,1)} %param.8), kind=kLoop, calls=%fused_computation | loop fusion | flops 128 | bytes 768 | tf_op jit(solution)/shard_map/transpose | solution.py:347
  1.2 115.0 %shard_map.64 = bf16[64,7168]{1,0:T(8,128)(2,1)} custom-call(bf16[64,7168]{1,0:T(8,128)(2,1)} %tokens.1, s32[2,64]{1,0:T(2,128)} %bitcast.3, f32[2,64]{1,0:T(2,128)} %convert_bitcast_fusion.gates_t, bf16[1,7168,1024]{2,1,0:T(8,128)(2,1)} %w_gate.1, bf16[1,7168,1024]{2,1,0:T(8,128)(2,1)} %w_up.1, bf16[1,1024,7168]{2,1,0:T(8,128)(2,1)} %w_down.1), custom_call_target="tpu_custom_call" | custom-call | flops 16911433728 | bytes 44040192 | tf_op jit(solution)/shard_map/pallas_call | solution.py:312
  116.2 2.2 %copy.8 = bf16[64,7168]{1,0:T(8,128)(2,1)} copy(bf16[64,7168]{1,0:T(8,128)(2,1)} %shard_map.64) | data formatting | bytes 1835008

commit v2 on v1

--- a/solution.py
+++ b/solution.py
@@ -16,8 +16,9 @@
 TILE = 512
 NT = (((1,), (1,)), ((), ()))
 
-TOK, TBL, OUT, Z, Y, C1, C2, RC, RY, RZ = 0, 1, 2, 4, 8, 12, 16, 20, 24, 28
-SEMS = 32
+TOK, TBL, OUT, Z, Y, C1, C2, RC, RY, RZ = 0, 1, 2, 4, 12, 20, 24, 28, 32, 40
+SEMS = 48
+SLOT = (1, 3, 2, 0)
 
 
 def fused_kernel(
@@ -136,130 +137,176 @@
             got += jnp.dot(s_nbr, tok_n[:, pl.ds(at, TILE)], preferred_element_type=F32)
             dst[:, pl.ds(at, TILE)] = got.astype(BF16)
 
-    def z_copy(k):
+    cut = half // 2
+    going = (pl.ds(0, cut), pl.ds(cut, half - cut + LANES))
+    coming = (pl.ds(0, cut), pl.ds(cut, half - cut))
+
+    def z_copy(k, p):
         return remote(
-            sendz.at[k - 1], x.at[c, me, y], Z + k, {"node": node_of[k]}
+            sendz.at[k - 1, :, going[p]],
+            x.at[c, SLOT[k], y, :, going[p]],
+            Z + 2 * k + p,
+            {"node": node_of[k]},
         )
 
-    def y_copy(k):
-        here = x.at[c, node_of[k], y]
-        return remote(here, here, Y + k, y_nbr)
+    def y_copy(k, p):
+        here = x.at[c, SLOT[k], y, :, going[p]]
+        return remote(here, here, Y + 2 * k + p, y_nbr)
 
     def c1_copy(k):
-        here = x.at[c, node_of[k], y]
+        here = x.at[c, SLOT[k], y]
         return remote(here, here, C1 + k, core_nbr)
 
     def c2_copy(k):
-        here = x.at[c, node_of[k], 1 - y]
+        here = x.at[c, SLOT[k], 1 - y]
         return remote(here, here, C2 + k, core_nbr)
 
     def rc_copy(k):
         return remote(
-            x.at[1 - c, node_of[k], :, :, pl.ds(0, half)], crecv.at[k], RC + k, core_nbr
+            x.at[1 - c, SLOT[k], :, :, pl.ds(0, half)], crecv.at[k], RC + k, core_nbr
         )
 
-    def ry_copy(k):
-        return remote(crecv.at[k, 1 - y], yrecv.at[k], RY + k, y_nbr)
-
-    def rz_copy(k):
-        return remote(crecv.at[k, y], zret.at[k], RZ + k, {"node": node_of[k]})
-
-    def take_z(k):
+    def ry_copy(k, p):
+        return remote(
+            crecv.at[k, 1 - y, :, coming[p]], yrecv.at[k, :, coming[p]], RY + 2 * k + p, y_nbr
+        )
+
+    def rz_copy(k, p):
+        return remote(
+            crecv.at[k, y, :, coming[p]],
+            zret.at[k, :, coming[p]],
+            RZ + 2 * k + p,
+            {"node": node_of[k]},
+        )
+
+    def take_z(k, p):
         if k > 0:
-            z_copy(k).wait_recv()
-        y_copy(k).start()
-        c1_copy(k).start()
+            z_copy(k, p).wait_recv()
+        y_copy(k, p).start()
+        if p == 1:
+            c1_copy(k).start()
 
     def take_y(k):
-        y_copy(k).wait_recv()
+        for p in range(2):
+            y_copy(k, p).wait_recv()
         c2_copy(k).start()
 
-    def compute(k):
-        m = node_of[k]
-        c1_copy(k).wait()
-        c2_copy(k).wait()
-        y_copy(k).wait_send()
-        count = 2 * pair
-        table = x[c, m, :, :, half : half + LANES].reshape(count, LANES).astype(F32)
+    count = 2 * 2 * pair
+
+    def up(rounds):
+        first = SLOT[rounds[0]]
+        both = pl.ds(first, 2)
+        for k in rounds:
+            c1_copy(k).wait_recv()
+            c2_copy(k).wait_recv()
+        table = x[c, both, :, :, half : half + LANES].reshape(count, LANES).astype(F32)
         mine = lax.broadcasted_iota(jnp.int32, (count, LANES), 1) == me * EXP_NODE + y
         weight = jnp.sum(jnp.where(mine, table, 0.0), axis=1, keepdims=True)
 
         @pl.loop(0, ff // GATE_TILE)
         def _(j):
             cols = pl.ds(pl.multiple_of(j * GATE_TILE, GATE_TILE), GATE_TILE)
-            x0 = x[0, m, :, :, :half].reshape(count, half)
-            x1 = x[1, m, :, :, :half].reshape(count, half)
+            x0 = x[0, both, :, :, :half].reshape(count, half)
+            x1 = x[1, both, :, :, :half].reshape(count, half)
             gate = jnp.dot(x0, wg[:half, cols], preferred_element_type=F32)
             gate += jnp.dot(x1, wg[half:, cols], preferred_element_type=F32)
             upper = jnp.dot(x0, wu[:half, cols], preferred_element_type=F32)
             upper += jnp.dot(x1, wu[half:, cols], preferred_element_type=F32)
             hid[:, cols] = (weight * (gate / (1.0 + jnp.exp(-gate))) * upper).astype(BF16)
 
-        for h in range(2):
-
-            @pl.loop(0, half // TILE)
-            def _(j):
-                at = pl.multiple_of(j * TILE, TILE)
-                part = jnp.dot(
-                    hid[...], wd[:, pl.ds(pl.multiple_of(h * half + at, TILE), TILE)],
-                    preferred_element_type=F32,
-                )
-                x[h, m, :, :, pl.ds(at, TILE)] = part.astype(BF16).reshape(2, pair, TILE)
-
-        rc_copy(k).start()
+    def down(rounds, h):
+        both = pl.ds(SLOT[rounds[0]], 2)
+
+        @pl.loop(0, half // TILE)
+        def _(j):
+            at = pl.multiple_of(j * TILE, TILE)
+            part = jnp.dot(
+                hid[...],
+                wd[:, pl.ds(pl.multiple_of(h * half + at, TILE), TILE)],
+                preferred_element_type=F32,
+            )
+            x[h, both, :, :, pl.ds(at, TILE)] = part.astype(BF16).reshape(2, 2, pair, TILE)
+
+    def down_nbr(rounds):
+        down(rounds, 1 - c)
+        for k in rounds:
+            rc_copy(k).start()
+
+    def down_own(rounds):
+        for k in rounds:
+            c1_copy(k).wait_send()
+            c2_copy(k).wait_send()
+            for p in range(2):
+                y_copy(k, p).wait_send()
+        down(rounds, c)
 
     def fold_core(k):
         rc_copy(k).wait_recv()
-        crecv[k, 1 - y] = (
-            crecv[k, 1 - y].astype(F32) + x[c, node_of[k], 1 - y, :, :half].astype(F32)
-        ).astype(BF16)
-        ry_copy(k).start()
+        for p in range(2):
+            cols = coming[p]
+            crecv[k, 1 - y, :, cols] = (
+                crecv[k, 1 - y, :, cols].astype(F32)
+                + x[c, SLOT[k], 1 - y, :, cols].astype(F32)
+            ).astype(BF16)
+            ry_copy(k, p).start()
 
     def fold_y(k):
-        ry_copy(k).wait_recv()
-        total = (
-            crecv[k, y].astype(F32)
-            + x[c, node_of[k], y, :, :half].astype(F32)
-            + yrecv[k].astype(F32)
-        ).astype(BF16)
-        if k == 0:
-            zret[0] = total
-        else:
-            crecv[k, y] = total
-            rz_copy(k).start()
-
-    build(2, sendz.at[1])
-    z_copy(2).start()
-    build(1, sendz.at[0])
-    z_copy(1).start()
-    build(0, x.at[c, me, y])
-    take_z(0)
+        for p in range(2):
+            cols = coming[p]
+            ry_copy(k, p).wait_recv()
+            total = (
+                crecv[k, y, :, cols].astype(F32)
+                + x[c, SLOT[k], y, :, cols].astype(F32)
+                + yrecv[k, :, cols].astype(F32)
+            ).astype(BF16)
+            if k == 0:
+                zret[0, :, cols] = total
+            else:
+                crecv[k, y, :, cols] = total
+                rz_copy(k, p).start()
+
+    build(3, sendz.at[2])
+    z_copy(3, 0).start()
+    z_copy(3, 1).start()
+    build(0, x.at[c, SLOT[0], y])
+    take_z(0, 0)
+    take_z(0, 1)
     for load in loads:
         load.start()
-    build(3, sendz.at[2])
+    build(2, sendz.at[1])
+    build(1, sendz.at[0])
+    take_z(3, 0)
+    z_copy(3, 0).wait_send()
+    z_copy(2, 0).start()
     take_y(0)
-    z_copy(2).wait_send()
-    z_copy(3).start()
-    take_z(1)
-    take_z(2)
+    take_z(3, 1)
+    z_copy(3, 1).wait_send()
+    z_copy(2, 1).start()
+    z_copy(1, 0).start()
+    z_copy(1, 1).start()
+    take_y(3)
     for load in loads:
         load.wait()
-    compute(0)
+    up((3, 0))
+    take_z(2, 0)
+    down_nbr((3, 0))
+    take_z(2, 1)
+    down_own((3, 0))
+    fold_core(3)
+    take_z(1, 0)
+    take_z(1, 1)
+    fold_y(3)
+    take_y(2)
     take_y(1)
-    take_y(2)
+    up((2, 1))
     fold_core(0)
-    compute(1)
-    take_z(3)
+    down_nbr((2, 1))
+    down_own((2, 1))
+    fold_core(2)
     fold_core(1)
     fold_y(0)
-    compute(2)
-    take_y(3)
-    fold_core(2)
+    fold_y(2)
     fold_y(1)
-    compute(3)
-    fold_y(2)
-    fold_core(3)
-    fold_y(3)
 
     eye = jnp.where(
         lax.broadcasted_iota(jnp.int32, (count_tok, count_tok), 0)
@@ -268,7 +315,8 @@
         0.0,
     ).astype(BF16)
     for k in (1, 2, 3):
-        rz_copy(k).wait_recv()
+        for p in range(2):
+            rz_copy(k, p).wait_recv()
     out_copy = remote(
         tok_n, out.at[:, pl.ds(own_at, half)], OUT, core_nbr
     )
@@ -290,13 +338,15 @@
     out_copy.wait()
     tok_copy.wait_send()
     tbl_copy.wait_send()
-    z_copy(1).wait_send()
-    z_copy(3).wait_send()
+    for p in range(2):
+        z_copy(1, p).wait_send()
+        z_copy(2, p).wait_send()
     for k in range(4):
         rc_copy(k).wait_send()
-        ry_copy(k).wait_send()
-        if k > 0:
-            rz_copy(k).wait_send()
+        for p in range(2):
+            ry_copy(k, p).wait_send()
+            if k > 0:
+                rz_copy(k, p).wait_send()
 
 
 def fused(tokens, expert_ids, gate_values, w_gate, w_up, w_down):
@@ -325,7 +375,7 @@
             pltpu.VMEM((8, count_tok), F32),
             pltpu.VMEM((8, count_tok), F32),
             pltpu.VMEM((2, nodes * pair, count_tok), BF16),
-            pltpu.VMEM((2 * pair, ff), BF16),
+            pltpu.VMEM((4 * pair, ff), BF16),
             pltpu.VMEM((nodes, 2, pair, half), BF16),
             pltpu.VMEM((nodes, pair, half), BF16),
             pltpu.VMEM((nodes, pair, half), BF16),

time: 119 us -> 120 us (level)
  the two profiles are of different devices: /device:TPU:21 before, /device:TPU:0 now
where the time goes in v2:
time: 120 us
  Pallas kernels  117 us (98%)
  local copies, waits for them, and re-layouts  2.16 us (2%)
  other arithmetic  1.22 us (1%)
    pallas_call x1, Pallas kernels, fused(): pl.pallas_call(functools.partial(fused_kernel, cap), out_shape=jax.ShapeD...  117 us

profile of v2, /device:TPU:0, one launch (start us, length us, event | category | flops | bytes accessed | tf_op | source)
XLA Modules:
  0.0 120.1 jit_solution(10218424101391716097)
XLA Ops:
  0.0 1.2 %convert_bitcast_fusion.gates_t = f32[2,64]{1,0:T(2,128)} fusion(bf16[64,2]{0,1:T(2,128)(2,1)} %param.8), kind=kLoop, calls=%fused_computation | loop fusion | flops 128 | bytes 768 | tf_op jit(solution)/shard_map/transpose | solution.py:397
  1.2 116.7 %shard_map.64 = bf16[64,7168]{1,0:T(8,128)(2,1)} custom-call(bf16[64,7168]{1,0:T(8,128)(2,1)} %tokens.1, s32[2,64]{1,0:T(2,128)} %bitcast.3, f32[2,64]{1,0:T(2,128)} %convert_bitcast_fusion.gates_t, bf16[1,7168,1024]{2,1,0:T(8,128)(2,1)} %w_gate.1, bf16[1,7168,1024]{2,1,0:T(8,128)(2,1)} %w_up.1, bf16[1,1024,7168]{2,1,0:T(8,128)(2,1)} %w_down.1), custom_call_target="tpu_custom_call" | custom-call | flops 16911433728 | bytes 44040192 | tf_op jit(solution)/shard_map/pallas_call | solution.py:362
  117.9 2.2 %copy.8 = bf16[64,7168]{1,0:T(8,128)(2,1)} copy(bf16[64,7168]{1,0:T(8,128)(2,1)} %shard_map.64) | data formatting | bytes 1835008

commit v3 on v2

--- a/solution.py
+++ b/solution.py
@@ -268,13 +268,15 @@
     build(3, sendz.at[2])
     z_copy(3, 0).start()
     z_copy(3, 1).start()
+    build(1, sendz.at[0])
+    z_copy(1, 0).start()
+    z_copy(1, 1).start()
     build(0, x.at[c, SLOT[0], y])
     take_z(0, 0)
     take_z(0, 1)
     for load in loads:
         load.start()
     build(2, sendz.at[1])
-    build(1, sendz.at[0])
     take_z(3, 0)
     z_copy(3, 0).wait_send()
     z_copy(2, 0).start()
@@ -282,27 +284,27 @@
     take_z(3, 1)
     z_copy(3, 1).wait_send()
     z_copy(2, 1).start()
-    z_copy(1, 0).start()
-    z_copy(1, 1).start()
+    take_z(1, 0)
+    take_z(1, 1)
     take_y(3)
     for load in loads:
         load.wait()
     up((3, 0))
+    take_y(1)
     take_z(2, 0)
     down_nbr((3, 0))
     take_z(2, 1)
     down_own((3, 0))
     fold_core(3)
-    take_z(1, 0)
-    take_z(1, 1)
+    take_y(2)
     fold_y(3)
-    take_y(2)
-    take_y(1)
+    fold_core(0)
     up((2, 1))
-    fold_core(0)
     down_nbr((2, 1))
     down_own((2, 1))
     fold_core(2)
+    for p in range(2):
+        ry_copy(2, p).wait_send()
     fold_core(1)
     fold_y(0)
     fold_y(2)
@@ -344,7 +346,8 @@
     for k in range(4):
         rc_copy(k).wait_send()
         for p in range(2):
-            ry_copy(k, p).wait_send()
+            if k != 2:
+                ry_copy(k, p).wait_send()
             if k > 0:
                 rz_copy(k, p).wait_send()
 

time: 120 us -> 106 us (0.88)
  Pallas kernels: 117 us -> 103 us
    pallas_call x1, Pallas kernels: 117 us -> 103 us  [fused(): pl.pallas_call(functools.partial(fused_kernel, cap), out_shape=jax.ShapeD...]
where the time goes in v3:
time: 106 us
  Pallas kernels  103 us (97%)
  local copies, waits for them, and re-layouts  2.16 us (2%)
  other arithmetic  1.22 us (1%)
    pallas_call x1, Pallas kernels, fused(): pl.pallas_call(functools.partial(fused_kernel, cap), out_shape=jax.ShapeD...  103 us
    unnamed x1, local copies, waits for them, and re-layouts  2.16 us

profile of v3, /device:TPU:0, one launch (start us, length us, event | category | flops | bytes accessed | tf_op | source)
XLA Modules:
  0.0 106.1 jit_solution(13425611371239418013)
XLA Ops:
  0.0 1.2 %convert_bitcast_fusion.gates_t = f32[2,64]{1,0:T(2,128)} fusion(bf16[64,2]{0,1:T(2,128)(2,1)} %param.8), kind=kLoop, calls=%fused_computation | loop fusion | flops 128 | bytes 768 | tf_op jit(solution)/shard_map/transpose | solution.py:400
  1.2 102.8 %shard_map.64 = bf16[64,7168]{1,0:T(8,128)(2,1)} custom-call(bf16[64,7168]{1,0:T(8,128)(2,1)} %tokens.1, s32[2,64]{1,0:T(2,128)} %bitcast.3, f32[2,64]{1,0:T(2,128)} %convert_bitcast_fusion.gates_t, bf16[1,7168,1024]{2,1,0:T(8,128)(2,1)} %w_gate.1, bf16[1,7168,1024]{2,1,0:T(8,128)(2,1)} %w_up.1, bf16[1,1024,7168]{2,1,0:T(8,128)(2,1)} %w_down.1), custom_call_target="tpu_custom_call" | custom-call | flops 16911433728 | bytes 44040192 | tf_op jit(solution)/shard_map/pallas_call | solution.py:365
  104.0 2.2 %copy.8 = bf16[64,7168]{1,0:T(8,128)(2,1)} copy(bf16[64,7168]{1,0:T(8,128)(2,1)} %shard_map.64) | data formatting | bytes 1835008
